TPU v7x, 32 devices: a whole 2x2x4 slice. The times are simulated.
32 devices in a mesh: grp: 2 (over y), gz: 8 (over z, x), gy: 2 (over core).
Axes of the slice: x: 2, y: 2, z: 4, core: 2. Of those that a mesh axis runs over, the one named last changes fastest.
Arguments:
- estimate_start: float32 [256, 64, 256], P(('grp', 'gz'), 'gy'), parts along dimension 0, may hold values from 0.5 to 2
- view_images: float32 [4, 256, 64, 256], P(None, ('grp', 'gz'), 'gy'), parts along dimension 1, may hold values from 0.5 to 2
- psf_taps: float32 [4, 3, 31], replicated, may hold values from 0.1 to 1
Outputs:
- estimate: float32 [256, 64, 256], P(('grp', 'gz'), 'gy'), parts along dimension 0
There are 2 independent parts, one for each index of `grp`. A program takes and returns all parts, laid end to end along the dimension named above; an argument that names none is the same for every part. Nothing has to cross between parts.
All inputs are finite; a program needn't handle non-finite values.
Results may differ from a plain program's by a relative error of at most 0.00022.
Values sent between devices are 32-bit elements; how exact they have to be, the bound alone decides.
No kernel may reach another device: no remote copies, remote signals or barrier semaphores. Data moves between devices by JAX's collectives and lax.ppermute only.
A program may use at most 64 MiB of HBM per device.

v0:
```python
import jax
import jax.numpy as jnp
from jax import lax
from jax.sharding import PartitionSpec as P

ITERS = 2


def with_halo(block, sides, width):
    for axis, dim in sides:
        count = lax.axis_size(axis)
        forward = [(i, i + 1) for i in range(count - 1)]
        backward = [(target, source) for source, target in forward]
        low = lax.ppermute(
            lax.slice_in_dim(block, block.shape[dim] - width, None, axis=dim), axis, forward
        )
        high = lax.ppermute(lax.slice_in_dim(block, 0, width, axis=dim), axis, backward)
        block = jnp.concatenate([low, block, high], axis=dim)
    return block


def band(kern, rows, cols, offset, sign):
    taps = kern.shape[0]
    row_ids = jnp.arange(rows, dtype=jnp.int32)[:, None]
    col_ids = jnp.arange(cols, dtype=jnp.int32)[None, :]
    diff = sign * (col_ids - row_ids) + offset
    total = jnp.zeros((rows, cols), kern.dtype)
    for tap in range(taps):
        total = total + jnp.where(diff == tap, kern[tap], 0.0)
    return total


def along_x(field, mat_x):
    return jnp.einsum("zyx,wx->zyw", field, mat_x, precision=lax.Precision.HIGHEST)


def along_y(field, mat_y, half):
    padded = with_halo(field, (("gy", 1),), half)
    return jnp.einsum("zpx,yp->zyx", padded, mat_y, precision=lax.Precision.HIGHEST)


def to_columns(field):
    planes, rows_dev, cols = field.shape
    flat = field.reshape(planes, rows_dev * cols)
    return lax.all_to_all(flat, "gz", split_axis=1, concat_axis=0, tiled=True)


def from_columns(pencil, shape):
    back = lax.all_to_all(pencil, "gz", split_axis=0, concat_axis=1, tiled=True)
    return back.reshape(shape)


def along_z(pencil, mat_z):
    block_len = mat_z.shape[0]
    depth, width = pencil.shape
    blocks = pencil.reshape(depth // block_len, block_len, width)
    padded = jnp.pad(blocks, ((1, 1), (0, 0), (0, 0)))
    stacked = jnp.concatenate((padded[:-2], padded[1:-1], padded[2:]), axis=1)
    result = jnp.einsum("zp,bpc->bzc", mat_z, stacked, precision=lax.Precision.HIGHEST)
    return result.reshape(depth, width)


def local(estimate_start, view_images, psf_taps):
    planes, rows_dev, cols = estimate_start.shape
    taps = psf_taps.shape[2]
    half = taps // 2
    gz_count = lax.axis_size("gz")
    group = max(1, 128 // planes)
    while gz_count % group != 0:
        group = group - 1
    block_len = planes * group
    estimate = estimate_start
    for view in range(psf_taps.shape[0]):
        kernels = psf_taps[view] / jnp.sum(psf_taps[view], axis=1, keepdims=True)
        mat_z = band(kernels[0], block_len, 3 * block_len, half - block_len, 1)
        mat_za = band(kernels[0], block_len, 3 * block_len, half + block_len, -1)
        mat_yf = band(kernels[1], rows_dev, rows_dev + 2 * half, 0, 1)
        mat_ya = band(kernels[1], rows_dev, rows_dev + 2 * half, 2 * half, -1)
        mat_x = band(kernels[2], cols, cols, half, 1)
        mat_xa = mat_x.T
        for step in range(ITERS):
            partial_blur = along_y(along_x(estimate, mat_x), mat_yf, half)
            blurred = from_columns(along_z(to_columns(partial_blur), mat_z), estimate.shape)
            ratio = view_images[view] / blurred
            partial_back = along_y(along_x(ratio, mat_xa), mat_ya, half)
            correction = from_columns(along_z(to_columns(partial_back), mat_za), estimate.shape)
            estimate = estimate * correction
    return estimate


def solution(mesh):
    return jax.shard_map(
        local,
        mesh=mesh,
        in_specs=(P(("grp", "gz"), "gy", None), P(None, ("grp", "gz"), "gy", None), P()),
        out_specs=P(("grp", "gz"), "gy", None),
        check_vma=False,
    )
```

profile of v0, /device:TPU:1, one launch (start us, length us, event | category | flops | bytes accessed | tf_op | source)
XLA Modules:
  0.0 1680.1 jit_solution(14323620589097416687)
XLA Ops:
  3.2 21.8 %convolution_bitcast_fusion = f32[16,32,256]{2,1,0:T(8,128)S(1)} fusion(f32[16,32,256]{2,1,0:T(8,128)} %param.3, f32[]{:T(128)} %bitcast.64, f32[]{:T(128)} %bitcast.63, f32[]{:T(128)} %bitcast.62, f32[]{:T(128)} %bitcast.61, f32[]{:T(128)} %bitcast.60, f32[]{:T(128)} %bitcast.59, f32[]{:T(128)} %bitcast.58, f32[]{:T(128)} %bitcast.57, f32[]{:T(128)} %bitcast.56, ...), kind=kOutput, calls=%fused_computation.80 | convolution fusion | flops 408813568 | bytes 1048700 | tf_op jit(solution)/shard_map/zyx,wx->zyw/dot_general | solution.py:34
  71.9 20.6 %fusion.1 = f32[1024,128]{0,1:T(8,128)S(1)} fusion(f32[1,128,1024]{2,1,0:T(8,128)S(1)} %slice.2306, f32[1,128,1024]{2,1,0:T(8,128)S(1)} %bitcast.726, f32[]{:T(128)} %bitcast.101, f32[]{:T(128)} %bitcast.100, f32[]{:T(128)} %bitcast.99, f32[]{:T(128)} %bitcast.98, f32[]{:T(128)} %bitcast.97, f32[]{:T(128)} %bitcast.96, f32[]{:T(128)} %bitcast.95, ...), kind=kOutput, calls=%fused_computation.33 | convolution fusion | flops 609386496 | bytes 1572988 | tf_op jit(solution)/shard_map/zp,bpc->bzc/dot_general | solution.py:59
  111.1 21.9 %fusion.150 = f32[16,32,256]{2,1,0:T(8,128)S(1)} fusion(f32[16,32,256]{2,1,0:T(8,128)S(1)} %reshape.1102, f32[4,16,32,256]{3,2,1,0:T(8,128)} %param.4, f32[]{:T(128)} %bitcast.64, f32[]{:T(128)} %bitcast.63, f32[]{:T(128)} %bitcast.62, f32[]{:T(128)} %bitcast.61, f32[]{:T(128)} %bitcast.60, f32[]{:T(128)} %bitcast.59, f32[]{:T(128)} %bitcast.58, ...), kind=kOutput, calls=%fused_computation.191 | convolution fusion | flops 408944640 | bytes 1588736 | tf_op jit(solution)/shard_map/zyx,wx->zyw/dot_general | solution.py:34
  176.6 21.0 %fusion.4 = f32[1024,128]{0,1:T(8,128)S(1)} fusion(f32[1,128,1024]{2,1,0:T(8,128)S(1)} %slice.2306, f32[1,128,1024]{2,1,0:T(8,128)S(1)} %bitcast.736, f32[]{:T(128)} %bitcast.101, f32[]{:T(128)} %bitcast.100, f32[]{:T(128)} %bitcast.99, f32[]{:T(128)} %bitcast.98, f32[]{:T(128)} %bitcast.97, f32[]{:T(128)} %bitcast.96, f32[]{:T(128)} %bitcast.95, ...), kind=kOutput, calls=%fused_computation.35 | convolution fusion | flops 609435648 | bytes 1572988 | tf_op jit(solution)/shard_map/zp,bpc->bzc/dot_general | solution.py:59
  216.2 20.7 %fusion.179 = f32[16,32,256]{2,1,0:T(8,128)S(1)} fusion(f32[16,32,256]{2,1,0:T(8,128)S(1)} %mul.530, f32[]{:T(128)} %bitcast.64, f32[]{:T(128)} %bitcast.63, f32[]{:T(128)} %bitcast.62, f32[]{:T(128)} %bitcast.61, f32[]{:T(128)} %bitcast.60, f32[]{:T(128)} %bitcast.59, f32[]{:T(128)} %bitcast.58, f32[]{:T(128)} %bitcast.57, f32[]{:T(128)} %bitcast.56, ...), kind=kOutput, calls=%fused_computation.220 | convolution fusion | flops 408813568 | bytes 1048700 | tf_op jit(solution)/shard_map/zyx,wx->zyw/dot_general | solution.py:34
  280.6 20.6 %fusion.7 = f32[1024,128]{0,1:T(8,128)S(1)} fusion(f32[1,128,1024]{2,1,0:T(8,128)S(1)} %slice.2306, f32[1,128,1024]{2,1,0:T(8,128)S(1)} %bitcast.738, f32[]{:T(128)} %bitcast.101, f32[]{:T(128)} %bitcast.100, f32[]{:T(128)} %bitcast.99, f32[]{:T(128)} %bitcast.98, f32[]{:T(128)} %bitcast.97, f32[]{:T(128)} %bitcast.96, f32[]{:T(128)} %bitcast.95, ...), kind=kOutput, calls=%fused_computation.37 | convolution fusion | flops 609386496 | bytes 1572988 | tf_op jit(solution)/shard_map/zp,bpc->bzc/dot_general | solution.py:59
  319.1 21.9 %fusion.151 = f32[16,32,256]{2,1,0:T(8,128)S(1)} fusion(f32[16,32,256]{2,1,0:T(8,128)S(1)} %reshape.1108, f32[4,16,32,256]{3,2,1,0:T(8,128)} %param.4, f32[]{:T(128)} %bitcast.64, f32[]{:T(128)} %bitcast.63, f32[]{:T(128)} %bitcast.62, f32[]{:T(128)} %bitcast.61, f32[]{:T(128)} %bitcast.60, f32[]{:T(128)} %bitcast.59, f32[]{:T(128)} %bitcast.58, ...), kind=kOutput, calls=%fused_computation.192 | convolution fusion | flops 408944640 | bytes 1588736 | tf_op jit(solution)/shard_map/zyx,wx->zyw/dot_general | solution.py:34
  384.7 21.8 %fusion.10 = f32[1024,128]{0,1:T(8,128)} fusion(f32[1,128,1024]{2,1,0:T(8,128)S(1)} %slice.2306, f32[1,128,1024]{2,1,0:T(8,128)S(1)} %bitcast.729, f32[]{:T(128)} %bitcast.101, f32[]{:T(128)} %bitcast.100, f32[]{:T(128)} %bitcast.99, f32[]{:T(128)} %bitcast.98, f32[]{:T(128)} %bitcast.97, f32[]{:T(128)} %bitcast.96, f32[]{:T(128)} %bitcast.95, ...), kind=kOutput, calls=%fused_computation.39 | convolution fusion | flops 609435648 | bytes 1572988 | tf_op jit(solution)/shard_map/zp,bpc->bzc/dot_general | solution.py:59
  424.6 20.7 %fusion.176 = f32[16,32,256]{2,1,0:T(8,128)S(1)} fusion(f32[16,32,256]{2,1,0:T(8,128)S(1)} %mul.531, f32[]{:T(128)} %bitcast.194, f32[]{:T(128)} %bitcast.193, f32[]{:T(128)} %bitcast.192, f32[]{:T(128)} %bitcast.191, f32[]{:T(128)} %bitcast.190, f32[]{:T(128)} %bitcast.189, f32[]{:T(128)} %bitcast.188, f32[]{:T(128)} %bitcast.187, f32[]{:T(128)} %bitcast.186, ...), kind=kOutput, calls=%fused_computation.217 | convolution fusion | flops 408813568 | bytes 1048700 | tf_op jit(solution)/shard_map/zyx,wx->zyw/dot_general | solution.py:34
  490.6 20.6 %fusion.13 = f32[1024,128]{0,1:T(8,128)S(1)} fusion(f32[1,128,1024]{2,1,0:T(8,128)S(1)} %slice.2306, f32[1,128,1024]{2,1,0:T(8,128)S(1)} %bitcast.730, f32[]{:T(128)} %bitcast.230, f32[]{:T(128)} %bitcast.229, f32[]{:T(128)} %bitcast.228, f32[]{:T(128)} %bitcast.227, f32[]{:T(128)} %bitcast.226, f32[]{:T(128)} %bitcast.225, f32[]{:T(128)} %bitcast.224, ...), kind=kOutput, calls=%fused_computation.41 | convolution fusion | flops 609386496 | bytes 1572988 | tf_op jit(solution)/shard_map/zp,bpc->bzc/dot_general | solution.py:59
  529.8 21.9 %fusion.148 = f32[16,32,256]{2,1,0:T(8,128)S(1)} fusion(f32[16,32,256]{2,1,0:T(8,128)S(1)} %reshape.1114, f32[4,16,32,256]{3,2,1,0:T(8,128)} %param.4, f32[]{:T(128)} %bitcast.194, f32[]{:T(128)} %bitcast.193, f32[]{:T(128)} %bitcast.192, f32[]{:T(128)} %bitcast.191, f32[]{:T(128)} %bitcast.190, f32[]{:T(128)} %bitcast.189, f32[]{:T(128)} %bitcast.188, ...), kind=kOutput, calls=%fused_computation.187 | convolution fusion | flops 408944640 | bytes 1588736 | tf_op jit(solution)/shard_map/zyx,wx->zyw/dot_general | solution.py:34
  595.3 21.0 %fusion.16 = f32[1024,128]{0,1:T(8,128)S(1)} fusion(f32[1,128,1024]{2,1,0:T(8,128)S(1)} %slice.2306, f32[1,128,1024]{2,1,0:T(8,128)S(1)} %bitcast.741, f32[]{:T(128)} %bitcast.230, f32[]{:T(128)} %bitcast.229, f32[]{:T(128)} %bitcast.228, f32[]{:T(128)} %bitcast.227, f32[]{:T(128)} %bitcast.226, f32[]{:T(128)} %bitcast.225, f32[]{:T(128)} %bitcast.224, ...), kind=kOutput, calls=%fused_computation.43 | convolution fusion | flops 609435648 | bytes 1572988 | tf_op jit(solution)/shard_map/zp,bpc->bzc/dot_general | solution.py:59
  634.5 20.7 %fusion.173 = f32[16,32,256]{2,1,0:T(8,128)S(1)} fusion(f32[16,32,256]{2,1,0:T(8,128)S(1)} %mul.532, f32[]{:T(128)} %bitcast.194, f32[]{:T(128)} %bitcast.193, f32[]{:T(128)} %bitcast.192, f32[]{:T(128)} %bitcast.191, f32[]{:T(128)} %bitcast.190, f32[]{:T(128)} %bitcast.189, f32[]{:T(128)} %bitcast.188, f32[]{:T(128)} %bitcast.187, f32[]{:T(128)} %bitcast.186, ...), kind=kOutput, calls=%fused_computation.214 | convolution fusion | flops 408813568 | bytes 1048700 | tf_op jit(solution)/shard_map/zyx,wx->zyw/dot_general | solution.py:34
  698.9 20.6 %fusion.19 = f32[1024,128]{0,1:T(8,128)S(1)} fusion(f32[1,128,1024]{2,1,0:T(8,128)S(1)} %slice.2306, f32[1,128,1024]{2,1,0:T(8,128)S(1)} %bitcast.743, f32[]{:T(128)} %bitcast.230, f32[]{:T(128)} %bitcast.229, f32[]{:T(128)} %bitcast.228, f32[]{:T(128)} %bitcast.227, f32[]{:T(128)} %bitcast.226, f32[]{:T(128)} %bitcast.225, f32[]{:T(128)} %bitcast.224, ...), kind=kOutput, calls=%fused_computation.45 | convolution fusion | flops 609386496 | bytes 1572988 | tf_op jit(solution)/shard_map/zp,bpc->bzc/dot_general | solution.py:59
  737.4 21.9 %fusion.149 = f32[16,32,256]{2,1,0:T(8,128)S(1)} fusion(f32[16,32,256]{2,1,0:T(8,128)S(1)} %reshape.1120, f32[4,16,32,256]{3,2,1,0:T(8,128)} %param.4, f32[]{:T(128)} %bitcast.194, f32[]{:T(128)} %bitcast.193, f32[]{:T(128)} %bitcast.192, f32[]{:T(128)} %bitcast.191, f32[]{:T(128)} %bitcast.190, f32[]{:T(128)} %bitcast.189, f32[]{:T(128)} %bitcast.188, ...), kind=kOutput, calls=%fused_computation.188 | convolution fusion | flops 408944640 | bytes 1588736 | tf_op jit(solution)/shard_map/zyx,wx->zyw/dot_general | solution.py:34
  803.0 21.8 %fusion.22 = f32[1024,128]{0,1:T(8,128)} fusion(f32[1,128,1024]{2,1,0:T(8,128)S(1)} %slice.2306, f32[1,128,1024]{2,1,0:T(8,128)S(1)} %bitcast.731, f32[]{:T(128)} %bitcast.230, f32[]{:T(128)} %bitcast.229, f32[]{:T(128)} %bitcast.228, f32[]{:T(128)} %bitcast.227, f32[]{:T(128)} %bitcast.226, f32[]{:T(128)} %bitcast.225, f32[]{:T(128)} %bitcast.224, ...), kind=kOutput, calls=%fused_computation.47 | convolution fusion | flops 609435648 | bytes 1572988 | tf_op jit(solution)/shard_map/zp,bpc->bzc/dot_general | solution.py:59
  843.1 20.7 %fusion.170 = f32[16,32,256]{2,1,0:T(8,128)S(1)} fusion(f32[16,32,256]{2,1,0:T(8,128)S(1)} %mul.533, f32[]{:T(128)} %bitcast.323, f32[]{:T(128)} %bitcast.322, f32[]{:T(128)} %bitcast.321, f32[]{:T(128)} %bitcast.320, f32[]{:T(128)} %bitcast.319, f32[]{:T(128)} %bitcast.318, f32[]{:T(128)} %bitcast.317, f32[]{:T(128)} %bitcast.316, f32[]{:T(128)} %bitcast.315, ...), kind=kOutput, calls=%fused_computation.211 | convolution fusion | flops 408813568 | bytes 1048700 | tf_op jit(solution)/shard_map/zyx,wx->zyw/dot_general | solution.py:34
  909.1 20.6 %fusion.25 = f32[1024,128]{0,1:T(8,128)S(1)} fusion(f32[1,128,1024]{2,1,0:T(8,128)S(1)} %slice.2306, f32[1,128,1024]{2,1,0:T(8,128)S(1)} %bitcast.732, f32[]{:T(128)} %bitcast.359, f32[]{:T(128)} %bitcast.358, f32[]{:T(128)} %bitcast.357, f32[]{:T(128)} %bitcast.356, f32[]{:T(128)} %bitcast.355, f32[]{:T(128)} %bitcast.354, f32[]{:T(128)} %bitcast.353, ...), kind=kOutput, calls=%fused_computation.49 | convolution fusion | flops 609386496 | bytes 1572988 | tf_op jit(solution)/shard_map/zp,bpc->bzc/dot_general | solution.py:59
  948.4 21.9 %fusion.146 = f32[16,32,256]{2,1,0:T(8,128)S(1)} fusion(f32[16,32,256]{2,1,0:T(8,128)S(1)} %reshape.1126, f32[4,16,32,256]{3,2,1,0:T(8,128)} %param.4, f32[]{:T(128)} %bitcast.323, f32[]{:T(128)} %bitcast.322, f32[]{:T(128)} %bitcast.321, f32[]{:T(128)} %bitcast.320, f32[]{:T(128)} %bitcast.319, f32[]{:T(128)} %bitcast.318, f32[]{:T(128)} %bitcast.317, ...), kind=kOutput, calls=%fused_computation.183 | convolution fusion | flops 408944640 | bytes 1588736 | tf_op jit(solution)/shard_map/zyx,wx->zyw/dot_general | solution.py:34
  1013.9 21.0 %fusion.28 = f32[1024,128]{0,1:T(8,128)S(1)} fusion(f32[1,128,1024]{2,1,0:T(8,128)S(1)} %slice.2306, f32[1,128,1024]{2,1,0:T(8,128)S(1)} %bitcast.746, f32[]{:T(128)} %bitcast.359, f32[]{:T(128)} %bitcast.358, f32[]{:T(128)} %bitcast.357, f32[]{:T(128)} %bitcast.356, f32[]{:T(128)} %bitcast.355, f32[]{:T(128)} %bitcast.354, f32[]{:T(128)} %bitcast.353, ...), kind=kOutput, calls=%fused_computation.51 | convolution fusion | flops 609435648 | bytes 1572988 | tf_op jit(solution)/shard_map/zp,bpc->bzc/dot_general | solution.py:59
  1053.0 20.7 %fusion.167 = f32[16,32,256]{2,1,0:T(8,128)S(1)} fusion(f32[16,32,256]{2,1,0:T(8,128)S(1)} %mul.534, f32[]{:T(128)} %bitcast.323, f32[]{:T(128)} %bitcast.322, f32[]{:T(128)} %bitcast.321, f32[]{:T(128)} %bitcast.320, f32[]{:T(128)} %bitcast.319, f32[]{:T(128)} %bitcast.318, f32[]{:T(128)} %bitcast.317, f32[]{:T(128)} %bitcast.316, f32[]{:T(128)} %bitcast.315, ...), kind=kOutput, calls=%fused_computation.208 | convolution fusion | flops 408813568 | bytes 1048700 | tf_op jit(solution)/shard_map/zyx,wx->zyw/dot_general | solution.py:34
  1117.4 20.6 %fusion.31 = f32[1024,128]{0,1:T(8,128)S(1)} fusion(f32[1,128,1024]{2,1,0:T(8,128)S(1)} %slice.2306, f32[1,128,1024]{2,1,0:T(8,128)S(1)} %bitcast.748, f32[]{:T(128)} %bitcast.359, f32[]{:T(128)} %bitcast.358, f32[]{:T(128)} %bitcast.357, f32[]{:T(128)} %bitcast.356, f32[]{:T(128)} %bitcast.355, f32[]{:T(128)} %bitcast.354, f32[]{:T(128)} %bitcast.353, ...), kind=kOutput, calls=%fused_computation.53 | convolution fusion | flops 609386496 | bytes 1572988 | tf_op jit(solution)/shard_map/zp,bpc->bzc/dot_general | solution.py:59
  1155.9 21.9 %fusion.147 = f32[16,32,256]{2,1,0:T(8,128)S(1)} fusion(f32[16,32,256]{2,1,0:T(8,128)S(1)} %reshape.1132, f32[4,16,32,256]{3,2,1,0:T(8,128)} %param.4, f32[]{:T(128)} %bitcast.323, f32[]{:T(128)} %bitcast.322, f32[]{:T(128)} %bitcast.321, f32[]{:T(128)} %bitcast.320, f32[]{:T(128)} %bitcast.319, f32[]{:T(128)} %bitcast.318, f32[]{:T(128)} %bitcast.317, ...), kind=kOutput, calls=%fused_computation.184 | convolution fusion | flops 408944640 | bytes 1588736 | tf_op jit(solution)/shard_map/zyx,wx->zyw/dot_general | solution.py:34
  1221.5 21.8 %fusion.34 = f32[1024,128]{0,1:T(8,128)} fusion(f32[1,128,1024]{2,1,0:T(8,128)S(1)} %slice.2306, f32[1,128,1024]{2,1,0:T(8,128)S(1)} %bitcast.733, f32[]{:T(128)} %bitcast.359, f32[]{:T(128)} %bitcast.358, f32[]{:T(128)} %bitcast.357, f32[]{:T(128)} %bitcast.356, f32[]{:T(128)} %bitcast.355, f32[]{:T(128)} %bitcast.354, f32[]{:T(128)} %bitcast.353, ...), kind=kOutput, calls=%fused_computation.55 | convolution fusion | flops 609435648 | bytes 1572988 | tf_op jit(solution)/shard_map/zp,bpc->bzc/dot_general | solution.py:59
  1261.4 20.7 %fusion.164 = f32[16,32,256]{2,1,0:T(8,128)S(1)} fusion(f32[16,32,256]{2,1,0:T(8,128)S(1)} %mul.535, f32[]{:T(128)} %bitcast.452, f32[]{:T(128)} %bitcast.451, f32[]{:T(128)} %bitcast.450, f32[]{:T(128)} %bitcast.449, f32[]{:T(128)} %bitcast.448, f32[]{:T(128)} %bitcast.447, f32[]{:T(128)} %bitcast.446, f32[]{:T(128)} %bitcast.445, f32[]{:T(128)} %bitcast.444, ...), kind=kOutput, calls=%fused_computation.205 | convolution fusion | flops 408813568 | bytes 1048700 | tf_op jit(solution)/shard_map/zyx,wx->zyw/dot_general | solution.py:34
  1327.4 20.6 %fusion.37 = f32[1024,128]{0,1:T(8,128)S(1)} fusion(f32[1,128,1024]{2,1,0:T(8,128)S(1)} %slice.2306, f32[1,128,1024]{2,1,0:T(8,128)S(1)} %bitcast.734, f32[]{:T(128)} %bitcast.488, f32[]{:T(128)} %bitcast.487, f32[]{:T(128)} %bitcast.486, f32[]{:T(128)} %bitcast.485, f32[]{:T(128)} %bitcast.484, f32[]{:T(128)} %bitcast.483, f32[]{:T(128)} %bitcast.482, ...), kind=kOutput, calls=%fused_computation.57 | convolution fusion | flops 609386496 | bytes 1572988 | tf_op jit(solution)/shard_map/zp,bpc->bzc/dot_general | solution.py:59
  1366.7 21.9 %fusion.144 = f32[16,32,256]{2,1,0:T(8,128)S(1)} fusion(f32[16,32,256]{2,1,0:T(8,128)S(1)} %reshape.1138, f32[4,16,32,256]{3,2,1,0:T(8,128)} %param.4, f32[]{:T(128)} %bitcast.452, f32[]{:T(128)} %bitcast.451, f32[]{:T(128)} %bitcast.450, f32[]{:T(128)} %bitcast.449, f32[]{:T(128)} %bitcast.448, f32[]{:T(128)} %bitcast.447, f32[]{:T(128)} %bitcast.446, ...), kind=kOutput, calls=%fused_computation.179 | convolution fusion | flops 408944640 | bytes 1588736 | tf_op jit(solution)/shard_map/zyx,wx->zyw/dot_general | solution.py:34
  1432.2 21.0 %fusion.40 = f32[1024,128]{0,1:T(8,128)S(1)} fusion(f32[1,128,1024]{2,1,0:T(8,128)S(1)} %slice.2306, f32[1,128,1024]{2,1,0:T(8,128)S(1)} %bitcast.751, f32[]{:T(128)} %bitcast.488, f32[]{:T(128)} %bitcast.487, f32[]{:T(128)} %bitcast.486, f32[]{:T(128)} %bitcast.485, f32[]{:T(128)} %bitcast.484, f32[]{:T(128)} %bitcast.483, f32[]{:T(128)} %bitcast.482, ...), kind=kOutput, calls=%fused_computation.59 | convolution fusion | flops 609435648 | bytes 1572988 | tf_op jit(solution)/shard_map/zp,bpc->bzc/dot_general | solution.py:59
  1471.4 20.7 %fusion.161 = f32[16,32,256]{2,1,0:T(8,128)S(1)} fusion(f32[16,32,256]{2,1,0:T(8,128)S(1)} %mul.536, f32[]{:T(128)} %bitcast.452, f32[]{:T(128)} %bitcast.451, f32[]{:T(128)} %bitcast.450, f32[]{:T(128)} %bitcast.449, f32[]{:T(128)} %bitcast.448, f32[]{:T(128)} %bitcast.447, f32[]{:T(128)} %bitcast.446, f32[]{:T(128)} %bitcast.445, f32[]{:T(128)} %bitcast.444, ...), kind=kOutput, calls=%fused_computation.202 | convolution fusion | flops 408813568 | bytes 1048700 | tf_op jit(solution)/shard_map/zyx,wx->zyw/dot_general | solution.py:34
  1535.8 20.6 %fusion.43 = f32[1024,128]{0,1:T(8,128)S(1)} fusion(f32[1,128,1024]{2,1,0:T(8,128)S(1)} %slice.2306, f32[1,128,1024]{2,1,0:T(8,128)S(1)} %bitcast.753, f32[]{:T(128)} %bitcast.488, f32[]{:T(128)} %bitcast.487, f32[]{:T(128)} %bitcast.486, f32[]{:T(128)} %bitcast.485, f32[]{:T(128)} %bitcast.484, f32[]{:T(128)} %bitcast.483, f32[]{:T(128)} %bitcast.482, ...), kind=kOutput, calls=%fused_computation.61 | convolution fusion | flops 609386496 | bytes 1572988 | tf_op jit(solution)/shard_map/zp,bpc->bzc/dot_general | solution.py:59
  1574.3 21.9 %fusion.145 = f32[16,32,256]{2,1,0:T(8,128)S(1)} fusion(f32[16,32,256]{2,1,0:T(8,128)S(1)} %reshape.1144, f32[4,16,32,256]{3,2,1,0:T(8,128)} %param.4, f32[]{:T(128)} %bitcast.452, f32[]{:T(128)} %bitcast.451, f32[]{:T(128)} %bitcast.450, f32[]{:T(128)} %bitcast.449, f32[]{:T(128)} %bitcast.448, f32[]{:T(128)} %bitcast.447, f32[]{:T(128)} %bitcast.446, ...), kind=kOutput, calls=%fused_computation.180 | convolution fusion | flops 408944640 | bytes 1588736 | tf_op jit(solution)/shard_map/zyx,wx->zyw/dot_general | solution.py:34
  1639.8 21.0 %fusion.46 = f32[1024,128]{0,1:T(8,128)S(1)} fusion(f32[1,128,1024]{2,1,0:T(8,128)S(1)} %slice.2306, f32[1,128,1024]{2,1,0:T(8,128)S(1)} %bitcast.727, f32[]{:T(128)} %bitcast.488, f32[]{:T(128)} %bitcast.487, f32[]{:T(128)} %bitcast.486, f32[]{:T(128)} %bitcast.485, f32[]{:T(128)} %bitcast.484, f32[]{:T(128)} %bitcast.483, f32[]{:T(128)} %bitcast.482, ...), kind=kOutput, calls=%fused_computation.63 | convolution fusion | flops 609435648 | bytes 1572988 | tf_op jit(solution)/shard_map/zp,bpc->bzc/dot_general | solution.py:59
  (233 shorter events, 1000.7 us)
Async XLA Ops:
  25.1 5.1 collective-permute-start
  51.8 20.0 %all-to-all-start = ((f32[16,8,1024]{2,0,1:T(8,128)}), f32[16,8,1024]{2,0,1:T(8,128)S(1)}, u32[]{:S(2)}, u32[]{:S(2)}) async-start(f32[16,8,1024]{2,0,1:T(8,128)} %copy.20), calls=%async_computation | async-start | bytes 1048576 | tf_op jit(solution)/shard_map/all_to_all | solution.py:45
  133.1 5.0 collective-permute-start.2
  237.0 5.1 collective-permute-start.4
  238.3 5.0 collective-permute-start.5
  341.1 5.1 collective-permute-start.6
  342.4 4.9 collective-permute-start.7
  406.5 17.6 %all-to-all-start.7 = ((f32[8,16,1024]{2,1,0:T(8,128)}), f32[8,16,1024]{2,1,0:T(8,128)S(1)}, u32[]{:S(2)}, u32[]{:S(2)}) async-start(f32[8,16,1024]{2,1,0:T(8,128)} %bitcast.128), calls=%async_computation.7 | async-start | bytes 1048576 | tf_op jit(solution)/shard_map/all_to_all | solution.py:49
  445.4 6.1 collective-permute-start.8
  446.7 5.2 collective-permute-start.9
  473.2 17.4 %all-to-all-start.8 = ((f32[16,8,1024]{2,0,1:T(8,128)}), f32[16,8,1024]{2,0,1:T(8,128)S(1)}, u32[]{:S(2)}, u32[]{:S(2)}) async-start(f32[16,8,1024]{2,0,1:T(8,128)} %copy.28), calls=%async_computation.8 | async-start | bytes 1048576 | tf_op jit(solution)/shard_map/all_to_all | solution.py:45
  551.8 5.0 collective-permute-start.10
  655.3 5.1 collective-permute-start.12
  759.4 5.1 collective-permute-start.14
  824.8 17.8 %all-to-all-start.15 = ((f32[8,16,1024]{2,1,0:T(8,128)}), f32[8,16,1024]{2,1,0:T(8,128)S(1)}, u32[]{:S(2)}, u32[]{:S(2)}) async-start(f32[8,16,1024]{2,1,0:T(8,128)} %bitcast.257), calls=%async_computation.15 | async-start | bytes 1048576 | tf_op jit(solution)/shard_map/all_to_all | solution.py:49
  863.9 6.1 collective-permute-start.16
  865.2 5.2 collective-permute-start.17
  891.7 17.4 %all-to-all-start.16 = ((f32[16,8,1024]{2,0,1:T(8,128)}), f32[16,8,1024]{2,0,1:T(8,128)S(1)}, u32[]{:S(2)}, u32[]{:S(2)}) async-start(f32[16,8,1024]{2,0,1:T(8,128)} %copy.36), calls=%async_computation.16 | async-start | bytes 1048576 | tf_op jit(solution)/shard_map/all_to_all | solution.py:45
  970.3 5.0 collective-permute-start.18
  1073.8 5.1 collective-permute-start.20
  1075.1 4.9 collective-permute-start.21
  1177.9 5.1 collective-permute-start.22
  1179.2 5.0 collective-permute-start.23
  1243.3 17.6 %all-to-all-start.23 = ((f32[8,16,1024]{2,1,0:T(8,128)}), f32[8,16,1024]{2,1,0:T(8,128)S(1)}, u32[]{:S(2)}, u32[]{:S(2)}) async-start(f32[8,16,1024]{2,1,0:T(8,128)} %bitcast.386), calls=%async_computation.23 | async-start | bytes 1048576 | tf_op jit(solution)/shard_map/all_to_all | solution.py:49
  1282.2 6.1 collective-permute-start.24
  1283.5 5.2 collective-permute-start.25
  1310.0 17.4 %all-to-all-start.24 = ((f32[16,8,1024]{2,0,1:T(8,128)}), f32[16,8,1024]{2,0,1:T(8,128)S(1)}, u32[]{:S(2)}, u32[]{:S(2)}) async-start(f32[16,8,1024]{2,0,1:T(8,128)} %copy.44), calls=%async_computation.24 | async-start | bytes 1048576 | tf_op jit(solution)/shard_map/all_to_all | solution.py:45
  1388.6 5.0 collective-permute-start.26
  1492.2 5.1 collective-permute-start.28
  1493.5 5.0 collective-permute-start.29
  1596.2 5.1 collective-permute-start.30
  1597.5 4.9 collective-permute-start.31
  (8 other events, 51.9 us)
where the time goes:
time: 1710 us; the launch traced here: 1680 us
  matrix products  998 us (58%)
  blocking collectives  433 us (25%)
  starting transfers between devices  112 us (7%)
  waiting for transfers between devices  99.8 us (6%)
  local copies, waits for them, and re-layouts  32.9 us (2%)
    dot_general x16, matrix products, along_x(): jnp.einsum('zyx,wx->zyw', field, mat_x, precision=lax.Precision.HIGHEST)  342 us
    dot_general x16, matrix products, along_z(): jnp.einsum('zp,bpc->bzc', mat_z, stacked, precision=lax.Precision.HIGHEST)  335 us
    dot_general x16, matrix products, along_y(): jnp.einsum('zpx,yp->zyx', padded, mat_y, precision=lax.Precision.HIGHEST)  320 us
    all_to_all x13, blocking collectives, from_columns(): back = lax.all_to_all(pencil, 'gz', split_axis=0, concat_axis=1, tiled=True)  231 us
    all_to_all x12, blocking collectives, to_columns(): return lax.all_to_all(flat, 'gz', split_axis=1, concat_axis=0, tiled=True)  203 us
    ppermute x16, starting transfers between devices, with_halo(): lax.ppermute(lax.slice_in_dim(block, 0, width, axis=dim), axis, backward)  60.6 us
    all_to_all x4, waiting for transfers between devices, to_columns(): return lax.all_to_all(flat, 'gz', split_axis=1, concat_axis=0, tiled=True)  51.6 us
  transfers between devices with their start and end apart: 39, of which 23 were waited for; matrix products, arithmetic and copies ran while one was open for 1% of the time, Pallas kernels for 0%

commit v1 on v0

v1 whole, which is shorter than its diff:
```python
import functools

import jax
import jax.numpy as jnp
from jax import lax
from jax.experimental import pallas as pl
from jax.experimental.pallas import tpu as pltpu
from jax.sharding import PartitionSpec as P

ITERS = 2
AXES = ("gz", "gy")
EDGE = 32
F32, BF16 = jnp.float32, jnp.bfloat16


def spot(zp, xp, c):
    return (2 * zp + xp) * 2 + c


def core_swap(n):
    return [(spot(z, x, c), spot(z, x, 1 - c)) for z in range(n) for x in range(2) for c in range(2)]


def half_swap(n):
    return [(spot(z, x, c), spot(z, 1 - x, c)) for z in range(n) for x in range(2) for c in range(2)]


def chip_swap(n):
    pairs = []
    for x in range(2):
        for z in range(n - 1):
            pairs += [(spot(z, x, 1), spot(z + 1, x, 0)), (spot(z + 1, x, 0), spot(z, x, 1))]
        pairs += [(spot(0, x, 0), spot(0, 1 - x, 0)), (spot(n - 1, x, 1), spot(n - 1, 1 - x, 1))]
    return pairs


def entry_one(n):
    pairs = []
    for z in range(n):
        pairs += [
            (spot(z, 0, 1), spot(z, 0, 0)),
            (spot(z, 0, 0), spot(z, 1, 0)),
            (spot(z, 1, 0), spot(z, 1, 1)),
            (spot(z, 1, 1), spot(z, 0, 1)),
        ]
    return pairs


def entry_two(n):
    pairs = []
    for z in range(n):
        pairs += [
            (spot(z, 0, 0), spot(z, 0, 0)),
            (spot(z, 0, 1), spot(z, 1, 0)),
            (spot(z, 1, 0), spot(z, 0, 1)),
            (spot(z, 1, 1), spot(z, 1, 1)),
        ]
    return pairs


def back(pairs):
    return [(target, source) for source, target in pairs]


def toeplitz(row, size):
    taps, row = row
    base = jnp.concatenate([row, jnp.zeros((1, size - row.shape[1]), F32)], axis=1) if size > row.shape[1] else row
    base = pltpu.roll(jnp.broadcast_to(base, (size, size)), size - taps // 2, 1)
    return pltpu.roll(base, 0, 1, stride=1, stride_axis=0)


def taps_row(taps_ref, index, taps):
    row = taps_ref[index : index + 1]
    return taps, row / jnp.sum(row, axis=1, keepdims=True)


def put_halves(ref, matrix):
    ref[0], ref[1] = split(matrix)


def lanes(shape, axis):
    return lax.broadcasted_iota(jnp.int32, shape, axis)


def mats_kernel(flags, taps_ref, xa_ref, x_ref, y_ref, ya_ref, z_ref, *, index, rows):
    size, wide = xa_ref.shape[1], x_ref.shape[2]
    taps = z_ref.shape[0]
    half = taps // 2
    first = flags[1] == 0

    def within(axis, width):
        lane = lanes((size, size), axis)
        low, high = jnp.where(first, wide + width, wide), jnp.where(first, size, size - width)
        return (lane < low) | (lane >= high)

    band_x = toeplitz(taps_row(taps_ref, index + 2, taps), size)
    held = jnp.where(within(0, EDGE) & within(1, half), band_x, 0.0)
    put_halves(xa_ref, held)
    kept = jnp.where(within(1, half), band_x, 0.0).T
    put_halves(x_ref, kept[:, :wide])
    band_y = toeplitz(taps_row(taps_ref, index + 1, taps), size)
    band_y = jnp.where(lanes((size, size), 0) // rows == lanes((size, size), 1) // rows, band_y, 0.0)
    put_halves(y_ref, band_y)
    put_halves(ya_ref, band_y.T)
    _, row = taps_row(taps_ref, index, taps)
    for tap in range(taps):
        z_ref[tap] = jnp.broadcast_to(row[:, tap : tap + 1], z_ref.shape[1:])


def split(value):
    high = value.astype(BF16)
    return high, (value - high.astype(F32)).astype(BF16)


def dot(a, b):
    return jnp.dot(a, b, preferred_element_type=F32)


def times_right(value, mat_ref):
    high, low = split(value)
    return dot(high, mat_ref[0]) + (dot(low, mat_ref[0]) + dot(high, mat_ref[1]))


def times_left(mat_ref, value):
    high, low = split(value)
    return dot(mat_ref[0], high) + (dot(mat_ref[0], low) + dot(mat_ref[1], high))


def call(kernel, outs, *args, scratch=()):
    def spec(a):
        small = a.ndim == 1
        return pl.BlockSpec(memory_space=pltpu.SMEM if small else pltpu.VMEM)

    return pl.pallas_call(
        kernel,
        out_shape=[jax.ShapeDtypeStruct(s, F32) if isinstance(s, tuple) else s for s in outs],
        in_specs=[spec(a) for a in args],
        out_specs=[pl.BlockSpec(memory_space=pltpu.VMEM) for _ in outs],
        scratch_shapes=list(scratch),
        compiler_params=pltpu.CompilerParams(vmem_limit_bytes=24 * 1024 * 1024),
    )(*args)


def blur_x_kernel(flags, taps_ref, est_ref, one_ref, two_ref, mat_ref, *, taps):
    planes, rows, cols = est_ref.shape
    wide = cols // 2
    band_x = toeplitz(taps_row(taps_ref, 2, taps), cols)
    near = jnp.abs(lanes((cols, cols), 0) - lanes((cols, cols), 1)) <= taps // 2
    put_halves(mat_ref, jnp.where(near, band_x, 0.0).T)
    group = 256 // rows
    lower = flags[0] == 0
    for g in range(planes // group):
        block = est_ref[group * g : group * (g + 1)].reshape(group * rows, cols)
        out = times_right(block, mat_ref)
        low, high = out[:, :wide].reshape(group, rows, wide), out[:, wide:].reshape(group, rows, wide)
        one_ref[group * g : group * (g + 1)] = jnp.where(lower, high, low)
        two_ref[group * g : group * (g + 1)] = jnp.where(lower, low, high)


def join_rows(flags, one_ref, two_ref, out_ref):
    rows = one_ref.shape[1]
    first = flags[1] == 0

    @pl.when(first)
    def _():
        out_ref[:, :rows] = two_ref[...]
        out_ref[:, rows:] = one_ref[...]

    @pl.when(jnp.logical_not(first))
    def _():
        out_ref[:, :rows] = one_ref[...]
        out_ref[:, rows:] = two_ref[...]


def blur_y_kernel(flags, one_ref, two_ref, mat_ref, out_ref):
    join_rows(flags, one_ref, two_ref, out_ref)
    planes, rows, cols = out_ref.shape
    size = mat_ref.shape[1]
    group = size // rows
    for g in range(planes // group):
        block = out_ref[group * g : group * (g + 1)].reshape(size, cols)
        out_ref[group * g : group * (g + 1)] = times_left(mat_ref, block).reshape(group, rows, cols)


def pack_edge(flags, blocks):
    first = jnp.where(flags[1] == 0, EDGE, 0)
    packed = None
    for g, block in enumerate(blocks):
        cols = block.shape[1]
        turned = pltpu.roll(block, (EDGE * g + first) % cols, 1)
        if packed is None:
            packed = turned
        else:
            lane = lax.broadcasted_iota(jnp.int32, block.shape, 1)
            packed = jnp.where(lane // EDGE == g, turned, packed)
    return packed


def open_edge(flags, packed, g):
    cols = packed.shape[1]
    first = jnp.where(flags[1] == 0, 0, cols - EDGE)
    return pltpu.roll(packed, (first + cols - EDGE * g) % cols, 1)


def enter_kernel(flags, one_ref, two_ref, main_ref, edge_ref):
    join_rows(flags, one_ref, two_ref, main_ref)
    planes, rows, cols = main_ref.shape
    groups = cols // EDGE
    each = planes // groups
    edge_ref[...] = pack_edge(
        flags, [main_ref[each * g : each * (g + 1)].reshape(each * rows, cols) for g in range(groups)]
    )


def extend_kernel(flags, main_ref, edge_ref, out_ref):
    planes, rows, cols = main_ref.shape
    groups = cols // EDGE
    each = planes // groups
    for g in range(groups):
        out_ref[each * rows * g : each * rows * (g + 1), :cols] = main_ref[
            each * g : each * (g + 1)
        ].reshape(each * rows, cols)
        out_ref[each * rows * g : each * rows * (g + 1), cols:] = open_edge(flags, edge_ref[...], g)


def update_kernel(flags, back_ref, edge_ref, est_ref, mat_xa, mat_x, mat_y, est_out, part_out):
    planes, rows, cols = back_ref.shape
    groups = cols // EDGE
    each = planes // groups
    size = each * rows
    for g in range(groups):
        at = slice(size * g, size * (g + 1))
        block = back_ref[each * g : each * (g + 1)].reshape(size, cols)
        wide = jnp.concatenate([block, open_edge(flags, edge_ref[...], g)], axis=1)
        est = est_ref[at] * times_right(wide, mat_xa)
        est_out[at] = est
        part = times_left(mat_y, times_right(est, mat_x))
        part_out[each * g : each * (g + 1)] = part.reshape(each, rows, cols)


def last_kernel(flags, back_ref, edge_ref, est_ref, mat_xa, one_out, two_out):
    planes, rows, cols = back_ref.shape
    groups = cols // EDGE
    each = planes // groups
    size = each * rows
    half = rows // 2
    first = flags[1] == 0
    for g in range(groups):
        at = slice(size * g, size * (g + 1))
        block = back_ref[each * g : each * (g + 1)].reshape(size, cols)
        wide = jnp.concatenate([block, open_edge(flags, edge_ref[...], g)], axis=1)
        est = (est_ref[at] * times_right(wide, mat_xa))[:, :cols].reshape(each, rows, cols)
        low, high = est[:, :half], est[:, half:]
        one_out[each * g : each * (g + 1)] = jnp.where(first, high, low)
        two_out[each * g : each * (g + 1)] = jnp.where(first, low, high)


def stack_planes(flags, own_ref, core_ref, chip_ref, stack):
    planes = own_ref.shape[0]
    core = flags[0]
    stack[planes : 2 * planes] = own_ref[...]
    stack[pl.ds((1 - core) * 2 * planes, planes)] = core_ref[...]

    @pl.when(flags[2] == 1)
    def _():
        stack[pl.ds(core * 2 * planes, planes)] = chip_ref[...]

    @pl.when(flags[2] == 0)
    def _():
        stack[pl.ds(core * 2 * planes, planes)] = jnp.zeros(chip_ref.shape, F32)


def along_z(taps_ref, stack, planes, at, flip):
    taps = taps_ref.shape[0]
    half = taps // 2
    field = [stack[planes - half + j, at, :] for j in range(planes + 2 * half)]
    total = [None] * planes
    for tap in range(taps):
        weight = taps_ref[taps - 1 - tap if flip else tap]
        for i in range(planes):
            term = weight * field[i + tap]
            total[i] = term if total[i] is None else total[i] + term
    return total


def ratio_kernel(flags, taps, own_ref, core_ref, chip_ref, one_ref, two_ref, out_ref, stack):
    planes, rows, _ = own_ref.shape
    half = rows // 2
    stack_planes(flags, own_ref, core_ref, chip_ref, stack)
    first = flags[1] == 0

    def step(i, carry):
        for side in range(2):
            at = pl.ds(pl.multiple_of(i * 8 + side * half, 8), 8)
            here = pl.ds(pl.multiple_of(i * 8, 8), 8)
            blurred = along_z(taps, stack, planes, at, False)
            for plane in range(planes):
                one, two = one_ref[plane, here, :], two_ref[plane, here, :]
                view = jnp.where(first, two, one) if side == 0 else jnp.where(first, one, two)
                out_ref[plane, at, :] = view / blurred[plane]
        return carry

    lax.fori_loop(0, half // 8, step, 0)


def back_kernel(flags, taps, own_ref, core_ref, chip_ref, mat_ref, out_ref, edge_ref, stack):
    planes, rows, cols = own_ref.shape
    stack_planes(flags, own_ref, core_ref, chip_ref, stack)

    def step(i, carry):
        at = pl.ds(pl.multiple_of(i * 8, 8), 8)
        total = along_z(taps, stack, planes, at, True)
        for plane in range(planes):
            out_ref[plane, at, :] = total[plane]
        return carry

    lax.fori_loop(0, rows // 8, step, 0)
    groups = cols // EDGE
    each = planes // groups
    blocks = []
    for g in range(groups):
        block = out_ref[each * g : each * (g + 1)].reshape(each * rows, cols)
        block = times_left(mat_ref, block)
        out_ref[each * g : each * (g + 1)] = block.reshape(each, rows, cols)
        blocks.append(block)
    edge_ref[...] = pack_edge(flags, blocks)


def local(estimate_start, view_images, psf_taps):
    planes, rows_dev, cols = estimate_start.shape
    views, _, taps = psf_taps.shape
    n = lax.axis_size("gz") // 2
    rows, wide = rows_dev * lax.axis_size("gy"), cols // 2
    zp, xp, core = lax.axis_index("gz") // 2, lax.axis_index("gz") % 2, lax.axis_index("gy")
    at_end = ((zp == 0) & (core == 0)) | ((zp == n - 1) & (core == 1))
    flags = jnp.stack([core, xp, jnp.where(at_end, 0, 1)]).astype(jnp.int32)
    send = lambda value, pairs: lax.ppermute(value, AXES, pairs)
    field = (planes, rows, wide)
    packed = (planes * rows * EDGE // wide, wide)
    piece = (planes, rows_dev, wide)
    stack = [pltpu.VMEM((3 * planes, rows, wide), F32)]

    rows_y = planes * rows * EDGE // wide
    table = jnp.pad(psf_taps.reshape(views * 3, taps), ((0, 0), (0, wide - taps)))

    def mats(view):
        pair = lambda n, m: jax.ShapeDtypeStruct((2, n, m), BF16)
        return call(
            functools.partial(mats_kernel, index=3 * view, rows=rows),
            [pair(cols, cols), pair(cols, wide), pair(rows_y, rows_y), pair(rows_y, rows_y), (taps, 8, wide)],
            flags, table,
        )

    def pieces(value):
        axis = value.ndim - 1
        return (
            lax.dynamic_slice_in_dim(value, wide * (1 - core), wide, axis),
            lax.dynamic_slice_in_dim(value, wide * core, wide, axis),
        )

    def enter(one, two):
        return send(one, entry_one(n)), send(two, entry_two(n))

    one, two = enter(
        *call(
            functools.partial(blur_x_kernel, taps=taps), [piece, piece], flags, table, estimate_start,
            scratch=[pltpu.VMEM((2, cols, cols), BF16)],
        )
    )
    mat_xa, mat_x, mat_y, mat_ya, k_z = mats(0)
    (part,) = call(blur_y_kernel, [field], flags, one, two, mat_y)
    images = [enter(*pieces(view_images[0]))]
    main, edge = call(enter_kernel, [field, packed], flags, *enter(*pieces(estimate_start)))
    edge = send(edge, half_swap(n))
    (estimate,) = call(extend_kernel, [(planes * rows, 2 * wide)], flags, main, edge)
    for view in range(1, views):
        images.append(enter(*pieces(view_images[view])))

    for view in range(views):
        one, two = images[view]
        for step in range(ITERS):
            ratio, = call(
                ratio_kernel, [field], flags, k_z, part,
                send(part, core_swap(n)), send(part, chip_swap(n)), one, two, scratch=stack,
            )
            corr, edge = call(
                back_kernel, [field, packed], flags, k_z, ratio,
                send(ratio, core_swap(n)), send(ratio, chip_swap(n)), mat_ya, scratch=stack,
            )
            edge = send(edge, half_swap(n))
            if step + 1 < ITERS:
                estimate, part = call(
                    update_kernel, [(planes * rows, 2 * wide), field], flags, corr, edge, estimate, mat_xa, mat_x, mat_y
                )
            elif view + 1 < views:
                old = mat_xa
                mat_xa, mat_x, mat_y, mat_ya, k_z = mats(view + 1)
                estimate, part = call(
                    update_kernel, [(planes * rows, 2 * wide), field], flags, corr, edge, estimate, old, mat_x, mat_y
                )
    one, two = call(last_kernel, [piece, piece], flags, corr, edge, estimate, mat_xa)
    one, two = send(one, back(entry_one(n))), send(two, back(entry_two(n)))
    return jnp.where(
        core == 0, jnp.concatenate([two, one], axis=2), jnp.concatenate([one, two], axis=2)
    )


def solution(mesh):
    return jax.shard_map(
        local,
        mesh=mesh,
        in_specs=(P(("grp", "gz"), "gy", None), P(None, ("grp", "gz"), "gy", None), P()),
        out_specs=P(("grp", "gz"), "gy", None),
        check_vma=False,
    )
```

time: 1710 us -> 312 us (0.18); the launches traced: 1680 us -> 310 us
  matrix products: 998 us -> 0 us
  blocking collectives: 433 us -> 0 us
  waiting for transfers between devices: 99.8 us -> 176 us
  Pallas kernels: 0 us -> 70.4 us
  starting transfers between devices: 112 us -> 56 us
  local copies, waits for them, and re-layouts: 32.9 us -> 5.91 us
    dot_general x48 -> x0, matrix products: 998 us -> none  [the longest x16 342 us: along_x(): jnp.einsum('zyx,wx->zyw', field, mat_x, precision=lax.Precision.HIGHEST)]
    all_to_all x25 -> x0, blocking collectives: 433 us -> none  [the longest x13 231 us: from_columns(): back = lax.all_to_all(pencil, 'gz', split_axis=0, concat_axis=1, tiled=True)]
    ppermute x32 -> x55, waiting for transfers between devices: 15.1 us -> 176 us  [local(): send = lambda value, pairs: lax.ppermute(value, AXES, pairs)]
    all_to_all x7 -> x0, waiting for transfers between devices: 84.8 us -> none  [the longest x4 51.6 us: to_columns(): return lax.all_to_all(flat, 'gz', split_axis=1, concat_axis=0, tiled=True)]
    pallas_call x0 -> x32, Pallas kernels: none -> 70.4 us  [call(): pl.pallas_call(kernel, out_shape=[jax.ShapeDtypeStruct(s, F32) if isinsta...]
    all_to_all x7 -> x0, starting transfers between devices: 30.8 us -> none  [the longest x4 17.6 us: to_columns(): return lax.all_to_all(flat, 'gz', split_axis=1, concat_axis=0, tiled=True)]
    ppermute x32 -> x55, starting transfers between devices: 81.3 us -> 56 us  [local(): send = lambda value, pairs: lax.ppermute(value, AXES, pairs)]
  transfers between devices with their start and end apart: 39 -> 55, of which waited for: 23 -> 44; matrix products, arithmetic and copies ran while one was open for 1% -> 1% of each run, Pallas kernels for 0% -> 3%
where the time goes in v1:
time: 312 us; the launch traced here: 310 us
  waiting for transfers between devices  176 us (56%)
  Pallas kernels  70.4 us (23%)
  starting transfers between devices  56 us (18%)
  local copies, waits for them, and re-layouts  5.91 us (2%)
    ppermute x55, waiting for transfers between devices, local(): send = lambda value, pairs: lax.ppermute(value, AXES, pairs)  176 us
    pallas_call x32, Pallas kernels, call(): pl.pallas_call(kernel, out_shape=[jax.ShapeDtypeStruct(s, F32) if isinsta...  70.4 us
    ppermute x55, starting transfers between devices, local(): send = lambda value, pairs: lax.ppermute(value, AXES, pairs)  56 us
  transfers between devices with their start and end apart: 55, of which 44 were waited for; matrix products, arithmetic and copies ran while one was open for 1% of the time, Pallas kernels for 3%

profile of v1, /device:TPU:1, one launch (start us, length us, event | category | flops | bytes accessed | tf_op | source)
XLA Modules:
  0.0 310.1 jit_solution(198044147284886914)
XLA Ops:
  3.2 4.5 %collective-permute-start.1 = (f32[16,32,128]{2,1,0:T(8,128)S(1)}, f32[16,32,128]{2,1,0:T(8,128)S(1)}, u32[]{:S(2)}, u32[]{:S(2)}) collective-permute-start(f32[16,32,128]{2,1,0:T(8,128)S(1)} %get-tuple-element.66), channel_id=1, source_target_pairs={{0,0},{1,2},{2,1},{3,3},{4,4},{5,6},{6,5},{7,7},{8,8},{9,10},{10,9... | collective-permute-start | bytes 786440 | tf_op jit(solution)/shard_map/ppermute | solution.py:337
  8.9 3.5 %collective-permute-done.1.two_ref = f32[16,32,128]{2,1,0:T(8,128)S(1)} collective-permute-done((f32[16,32,128]{2,1,0:T(8,128)S(1)}, f32[16,32,128]{2,1,0:T(8,128)S(1)}, u32[]{:S(2)}, u32[]{:S(2)}) %collective-permute-start.1) | collective-permute-done | bytes 262176 | tf_op jit(solution)/shard_map/ppermute | solution.py:337
  35.2 10.5 %collective-permute-done.10.two_ref = f32[16,32,128]{2,1,0:T(8,128)S(1)} collective-permute-done((f32[16,32,128]{2,1,0:T(8,128)S(1)}, f32[16,32,128]{2,1,0:T(8,128)S(1)}, u32[]{:S(2)}, u32[]{:S(2)}) %collective-permute-start.10) | collective-permute-done | bytes 262176 | tf_op jit(solution)/shard_map/ppermute | solution.py:337
  56.6 3.8 %collective-permute-start.12 = (f32[16,64,128]{2,1,0:T(8,128)S(1)}, f32[16,64,128]{2,1,0:T(8,128)S(1)}, u32[]{:S(2)}, u32[]{:S(2)}) collective-permute-start(f32[16,64,128]{2,1,0:T(8,128)S(1)} %get-tuple-element.75.own_ref), channel_id=1, source_target_pairs={{0,1},{1,0},{2,3},{3,2},{4,5},{5,4},{6,7},{7,6},{8,9},{9,8},{10,11... | collective-permute-start | bytes 1572872 | tf_op jit(solution)/shard_map/ppermute | solution.py:337
  61.9 7.3 %collective-permute-done.13.chip_ref = f32[16,64,128]{2,1,0:T(8,128)S(1)} collective-permute-done((f32[16,64,128]{2,1,0:T(8,128)S(1)}, f32[16,64,128]{2,1,0:T(8,128)S(1)}, u32[]{:S(2)}, u32[]{:S(2)}) %collective-permute-start.13) | collective-permute-done | bytes 524320 | tf_op jit(solution)/shard_map/ppermute | solution.py:337
  73.2 7.4 %collective-permute-done.15.chip_ref = f32[16,64,128]{2,1,0:T(8,128)S(1)} collective-permute-done((f32[16,64,128]{2,1,0:T(8,128)S(1)}, f32[16,64,128]{2,1,0:T(8,128)S(1)}, u32[]{:S(2)}, u32[]{:S(2)}) %collective-permute-start.15) | collective-permute-done | bytes 524320 | tf_op jit(solution)/shard_map/ppermute | solution.py:337
  84.3 3.6 %collective-permute-done.16.edge_ref = f32[256,128]{1,0:T(8,128)S(1)} collective-permute-done((f32[256,128]{1,0:T(8,128)S(1)}, f32[256,128]{1,0:T(8,128)S(1)}, u32[]{:S(2)}, u32[]{:S(2)}) %collective-permute-start.16) | collective-permute-done | bytes 131104 | tf_op jit(solution)/shard_map/ppermute | solution.py:337
  87.9 3.5 %shard_map.50 = (f32[1024,256]{1,0:T(8,128)S(1)}, f32[16,64,128]{2,1,0:T(8,128)S(1)}) custom-call(s32[3]{0:T(128)S(1)} %pad_add_fusion.flags, f32[16,64,128]{2,1,0:T(8,128)S(1)} %get-tuple-element.76.back_ref, f32[256,128]{1,0:T(8,128)S(1)} %collective-permute-done.16.edge_ref, f32[1024,256]{1,0:T(8,128)S(1)} %get-tuple-element.78.est_ref, ...), custom_call_target="tpu_custom_call" | custom-call | tf_op jit(solution)/shard_map/pallas_call | solution.py:134
  96.3 4.3 %collective-permute-done.19.one_ref = f32[16,32,128]{2,1,0:T(8,128)S(1)} collective-permute-done((f32[16,32,128]{2,1,0:T(8,128)S(1)}, f32[16,32,128]{2,1,0:T(8,128)S(1)}, u32[]{:S(2)}, u32[]{:S(2)}) %collective-permute-start.19) | collective-permute-done | bytes 262176 | tf_op jit(solution)/shard_map/ppermute | solution.py:337
  100.6 5.7 %collective-permute-done.20.two_ref = f32[16,32,128]{2,1,0:T(8,128)S(1)} collective-permute-done((f32[16,32,128]{2,1,0:T(8,128)S(1)}, f32[16,32,128]{2,1,0:T(8,128)S(1)}, u32[]{:S(2)}, u32[]{:S(2)}) %collective-permute-start.20) | collective-permute-done | bytes 262176 | tf_op jit(solution)/shard_map/ppermute | solution.py:337
  110.3 7.1 %collective-permute-done.22.chip_ref = f32[16,64,128]{2,1,0:T(8,128)S(1)} collective-permute-done((f32[16,64,128]{2,1,0:T(8,128)S(1)}, f32[16,64,128]{2,1,0:T(8,128)S(1)}, u32[]{:S(2)}, u32[]{:S(2)}) %collective-permute-start.22) | collective-permute-done | bytes 524320 | tf_op jit(solution)/shard_map/ppermute | solution.py:337
  124.5 3.5 %shard_map.53 = (f32[1024,256]{1,0:T(8,128)S(1)}, f32[16,64,128]{2,1,0:T(8,128)S(1)}) custom-call(s32[3]{0:T(128)S(1)} %pad_add_fusion.flags, f32[16,64,128]{2,1,0:T(8,128)S(1)} %get-tuple-element.83.back_ref, f32[256,128]{1,0:T(8,128)S(1)} %collective-permute-done.23.edge_ref, f32[1024,256]{1,0:T(8,128)S(1)} %get-tuple-element.85.est_ref, ...), custom_call_target="tpu_custom_call" | custom-call | tf_op jit(solution)/shard_map/pallas_call | solution.py:134
  131.2 7.3 %collective-permute-done.25.chip_ref = f32[16,64,128]{2,1,0:T(8,128)S(1)} collective-permute-done((f32[16,64,128]{2,1,0:T(8,128)S(1)}, f32[16,64,128]{2,1,0:T(8,128)S(1)}, u32[]{:S(2)}, u32[]{:S(2)}) %collective-permute-start.25) | collective-permute-done | bytes 524320 | tf_op jit(solution)/shard_map/ppermute | solution.py:337
  142.5 7.4 %collective-permute-done.27.chip_ref = f32[16,64,128]{2,1,0:T(8,128)S(1)} collective-permute-done((f32[16,64,128]{2,1,0:T(8,128)S(1)}, f32[16,64,128]{2,1,0:T(8,128)S(1)}, u32[]{:S(2)}, u32[]{:S(2)}) %collective-permute-start.27) | collective-permute-done | bytes 524320 | tf_op jit(solution)/shard_map/ppermute | solution.py:337
  157.2 3.5 %shard_map.56 = (f32[1024,256]{1,0:T(8,128)S(1)}, f32[16,64,128]{2,1,0:T(8,128)S(1)}) custom-call(s32[3]{0:T(128)S(1)} %pad_add_fusion.flags, f32[16,64,128]{2,1,0:T(8,128)S(1)} %get-tuple-element.88.back_ref, f32[256,128]{1,0:T(8,128)S(1)} %collective-permute-done.28.edge_ref, f32[1024,256]{1,0:T(8,128)S(1)} %get-tuple-element.90.est_ref, ...), custom_call_target="tpu_custom_call" | custom-call | tf_op jit(solution)/shard_map/pallas_call | solution.py:134
  165.7 4.3 %collective-permute-done.31.one_ref = f32[16,32,128]{2,1,0:T(8,128)S(1)} collective-permute-done((f32[16,32,128]{2,1,0:T(8,128)S(1)}, f32[16,32,128]{2,1,0:T(8,128)S(1)}, u32[]{:S(2)}, u32[]{:S(2)}) %collective-permute-start.31) | collective-permute-done | bytes 262176 | tf_op jit(solution)/shard_map/ppermute | solution.py:337
  170.0 5.7 %collective-permute-done.32.two_ref = f32[16,32,128]{2,1,0:T(8,128)S(1)} collective-permute-done((f32[16,32,128]{2,1,0:T(8,128)S(1)}, f32[16,32,128]{2,1,0:T(8,128)S(1)}, u32[]{:S(2)}, u32[]{:S(2)}) %collective-permute-start.32) | collective-permute-done | bytes 262176 | tf_op jit(solution)/shard_map/ppermute | solution.py:337
  179.7 7.1 %collective-permute-done.34.chip_ref = f32[16,64,128]{2,1,0:T(8,128)S(1)} collective-permute-done((f32[16,64,128]{2,1,0:T(8,128)S(1)}, f32[16,64,128]{2,1,0:T(8,128)S(1)}, u32[]{:S(2)}, u32[]{:S(2)}) %collective-permute-start.34) | collective-permute-done | bytes 524320 | tf_op jit(solution)/shard_map/ppermute | solution.py:337
  191.5 3.5 %collective-permute-done.35.edge_ref = f32[256,128]{1,0:T(8,128)S(1)} collective-permute-done((f32[256,128]{1,0:T(8,128)S(1)}, f32[256,128]{1,0:T(8,128)S(1)}, u32[]{:S(2)}, u32[]{:S(2)}) %collective-permute-start.35) | collective-permute-done | bytes 131104 | tf_op jit(solution)/shard_map/ppermute | solution.py:337
  195.0 3.5 %shard_map.59 = (f32[1024,256]{1,0:T(8,128)S(1)}, f32[16,64,128]{2,1,0:T(8,128)S(1)}) custom-call(s32[3]{0:T(128)S(1)} %pad_add_fusion.flags, f32[16,64,128]{2,1,0:T(8,128)S(1)} %get-tuple-element.95.back_ref, f32[256,128]{1,0:T(8,128)S(1)} %collective-permute-done.35.edge_ref, f32[1024,256]{1,0:T(8,128)S(1)} %get-tuple-element.97.est_ref, ...), custom_call_target="tpu_custom_call" | custom-call | tf_op jit(solution)/shard_map/pallas_call | solution.py:134
  201.0 7.3 %collective-permute-done.37.chip_ref = f32[16,64,128]{2,1,0:T(8,128)S(1)} collective-permute-done((f32[16,64,128]{2,1,0:T(8,128)S(1)}, f32[16,64,128]{2,1,0:T(8,128)S(1)}, u32[]{:S(2)}, u32[]{:S(2)}) %collective-permute-start.37) | collective-permute-done | bytes 524320 | tf_op jit(solution)/shard_map/ppermute | solution.py:337
  212.6 7.4 %collective-permute-done.39.chip_ref = f32[16,64,128]{2,1,0:T(8,128)S(1)} collective-permute-done((f32[16,64,128]{2,1,0:T(8,128)S(1)}, f32[16,64,128]{2,1,0:T(8,128)S(1)}, u32[]{:S(2)}, u32[]{:S(2)}) %collective-permute-start.39) | collective-permute-done | bytes 524320 | tf_op jit(solution)/shard_map/ppermute | solution.py:337
  227.2 3.5 %shard_map.62 = (f32[1024,256]{1,0:T(8,128)S(1)}, f32[16,64,128]{2,1,0:T(8,128)S(1)}) custom-call(s32[3]{0:T(128)S(1)} %pad_add_fusion.flags, f32[16,64,128]{2,1,0:T(8,128)S(1)} %get-tuple-element.100.back_ref, f32[256,128]{1,0:T(8,128)S(1)} %collective-permute-done.40.edge_ref, f32[1024,256]{1,0:T(8,128)S(1)} %get-tuple-element.102.est_ref, ...), custom_call_target="tpu_custom_call" | custom-call | tf_op jit(solution)/shard_map/pallas_call | solution.py:134
  235.9 4.2 %collective-permute-done.43.one_ref = f32[16,32,128]{2,1,0:T(8,128)S(1)} collective-permute-done((f32[16,32,128]{2,1,0:T(8,128)S(1)}, f32[16,32,128]{2,1,0:T(8,128)S(1)}, u32[]{:S(2)}, u32[]{:S(2)}) %collective-permute-start.43) | collective-permute-done | bytes 262176 | tf_op jit(solution)/shard_map/ppermute | solution.py:337
  240.0 5.7 %collective-permute-done.44.two_ref = f32[16,32,128]{2,1,0:T(8,128)S(1)} collective-permute-done((f32[16,32,128]{2,1,0:T(8,128)S(1)}, f32[16,32,128]{2,1,0:T(8,128)S(1)}, u32[]{:S(2)}, u32[]{:S(2)}) %collective-permute-start.44) | collective-permute-done | bytes 262176 | tf_op jit(solution)/shard_map/ppermute | solution.py:337
  249.8 7.4 %collective-permute-done.46.chip_ref = f32[16,64,128]{2,1,0:T(8,128)S(1)} collective-permute-done((f32[16,64,128]{2,1,0:T(8,128)S(1)}, f32[16,64,128]{2,1,0:T(8,128)S(1)}, u32[]{:S(2)}, u32[]{:S(2)}) %collective-permute-start.46) | collective-permute-done | bytes 524320 | tf_op jit(solution)/shard_map/ppermute | solution.py:337
  261.9 3.5 %collective-permute-done.47.edge_ref = f32[256,128]{1,0:T(8,128)S(1)} collective-permute-done((f32[256,128]{1,0:T(8,128)S(1)}, f32[256,128]{1,0:T(8,128)S(1)}, u32[]{:S(2)}, u32[]{:S(2)}) %collective-permute-start.47) | collective-permute-done | bytes 131104 | tf_op jit(solution)/shard_map/ppermute | solution.py:337
  265.5 3.5 %shard_map.65 = (f32[1024,256]{1,0:T(8,128)S(1)}, f32[16,64,128]{2,1,0:T(8,128)S(1)}) custom-call(s32[3]{0:T(128)S(1)} %pad_add_fusion.flags, f32[16,64,128]{2,1,0:T(8,128)S(1)} %get-tuple-element.107.back_ref, f32[256,128]{1,0:T(8,128)S(1)} %collective-permute-done.47.edge_ref, f32[1024,256]{1,0:T(8,128)S(1)} %get-tuple-element.109.est_ref, ...), custom_call_target="tpu_custom_call" | custom-call | tf_op jit(solution)/shard_map/pallas_call | solution.py:134
  271.5 7.3 %collective-permute-done.49.chip_ref = f32[16,64,128]{2,1,0:T(8,128)S(1)} collective-permute-done((f32[16,64,128]{2,1,0:T(8,128)S(1)}, f32[16,64,128]{2,1,0:T(8,128)S(1)}, u32[]{:S(2)}, u32[]{:S(2)}) %collective-permute-start.49) | collective-permute-done | bytes 524320 | tf_op jit(solution)/shard_map/ppermute | solution.py:337
  282.8 7.4 %collective-permute-done.51.chip_ref = f32[16,64,128]{2,1,0:T(8,128)S(1)} collective-permute-done((f32[16,64,128]{2,1,0:T(8,128)S(1)}, f32[16,64,128]{2,1,0:T(8,128)S(1)}, u32[]{:S(2)}, u32[]{:S(2)}) %collective-permute-start.51) | collective-permute-done | bytes 524320 | tf_op jit(solution)/shard_map/ppermute | solution.py:337
  298.7 4.5 %collective-permute-start.53 = (f32[16,32,128]{2,1,0:T(8,128)S(1)}, f32[16,32,128]{2,1,0:T(8,128)S(1)}, u32[]{:S(2)}, u32[]{:S(2)}) collective-permute-start(f32[16,32,128]{2,1,0:T(8,128)S(1)} %get-tuple-element.115), channel_id=1, source_target_pairs={{0,0},{2,1},{1,2},{3,3},{4,4},{6,5},{5,6},{7,7},{8,8},{10,9},{9,10... | collective-permute-start | bytes 786440 | tf_op jit(solution)/shard_map/ppermute | solution.py:337
  303.2 4.0 %collective-permute-done.53 = f32[16,32,128]{2,1,0:T(8,128)S(1)} collective-permute-done((f32[16,32,128]{2,1,0:T(8,128)S(1)}, f32[16,32,128]{2,1,0:T(8,128)S(1)}, u32[]{:S(2)}, u32[]{:S(2)}) %collective-permute-start.53) | collective-permute-done | bytes 262176 | tf_op jit(solution)/shard_map/ppermute | solution.py:337
  (131 shorter events, 137.2 us)
Async XLA Ops:
  3.2 9.2 %collective-permute-start.1 = (f32[16,32,128]{2,1,0:T(8,128)S(1)}, f32[16,32,128]{2,1,0:T(8,128)S(1)}, u32[]{:S(2)}, u32[]{:S(2)}) collective-permute-start(f32[16,32,128]{2,1,0:T(8,128)S(1)} %get-tuple-element.66), channel_id=1, source_target_pairs={{0,0},{1,2},{2,1},{3,3},{4,4},{5,6},{6,5},{7,7},{8,8},{9,10},{10,9... | collective-permute-start | bytes 786440 | tf_op jit(solution)/shard_map/ppermute | solution.py:337
  13.6 15.1 %collective-permute-start.2 = (f32[16,64,128]{2,1,0:T(8,128)S(1)}, f32[16,64,128]{2,1,0:T(8,128)S(1)}, u32[]{:S(2)}, u32[]{:S(2)}) collective-permute-start(f32[16,64,128]{2,1,0:T(8,128)S(1)} %shard_map.42.own_ref), channel_id=1, source_target_pairs={{0,1},{1,0},{2,3},{3,2},{4,5},{5,4},{6,7},{7,6},{8,9},{9,8},{10,11... | collective-permute-start | bytes 1572872 | tf_op jit(solution)/shard_map/ppermute | solution.py:337
  13.7 15.0 %collective-permute-start.3 = (f32[16,64,128]{2,1,0:T(8,128)S(1)}, f32[16,64,128]{2,1,0:T(8,128)S(1)}, u32[]{:S(2)}, u32[]{:S(2)}) collective-permute-start(f32[16,64,128]{2,1,0:T(8,128)S(1)} %shard_map.42.own_ref), channel_id=1, source_target_pairs={{1,4},{4,1},{5,8},{8,5},{9,12},{12,9},{0,2},{13,15},{3,6},{6,3},{7... | collective-permute-start | bytes 1572872 | tf_op jit(solution)/shard_map/ppermute | solution.py:337
  20.6 8.1 %collective-permute-start.5 = (f32[16,32,128]{2,1,0:T(8,128)S(1)}, f32[16,32,128]{2,1,0:T(8,128)S(1)}, u32[]{:S(2)}, u32[]{:S(2)}) collective-permute-start(f32[16,32,128]{2,1,0:T(8,128)S(1)} %get-tuple-element.129), channel_id=1, source_target_pairs={{0,0},{1,2},{2,1},{3,3},{4,4},{5,6},{6,5},{7,7},{8,8},{9,10},{10,9... | collective-permute-start | bytes 786440 | tf_op jit(solution)/shard_map/ppermute | solution.py:337
  30.7 15.8 %collective-permute-start.6 = (f32[16,64,128]{2,1,0:T(8,128)S(1)}, f32[16,64,128]{2,1,0:T(8,128)S(1)}, u32[]{:S(2)}, u32[]{:S(2)}) collective-permute-start(f32[16,64,128]{2,1,0:T(8,128)S(1)} %shard_map.43.own_ref), channel_id=1, source_target_pairs={{0,1},{1,0},{2,3},{3,2},{4,5},{5,4},{6,7},{7,6},{8,9},{9,8},{10,11... | collective-permute-start | bytes 1572872 | tf_op jit(solution)/shard_map/ppermute | solution.py:337
  30.8 15.8 %collective-permute-start.7 = (f32[16,64,128]{2,1,0:T(8,128)S(1)}, f32[16,64,128]{2,1,0:T(8,128)S(1)}, u32[]{:S(2)}, u32[]{:S(2)}) collective-permute-start(f32[16,64,128]{2,1,0:T(8,128)S(1)} %shard_map.43.own_ref), channel_id=1, source_target_pairs={{1,4},{4,1},{5,8},{8,5},{9,12},{12,9},{0,2},{13,15},{3,6},{6,3},{7... | collective-permute-start | bytes 1572872 | tf_op jit(solution)/shard_map/ppermute | solution.py:337
  31.9 13.7 %collective-permute-start.10 = (f32[16,32,128]{2,1,0:T(8,128)S(1)}, f32[16,32,128]{2,1,0:T(8,128)S(1)}, u32[]{:S(2)}, u32[]{:S(2)}) collective-permute-start(f32[16,32,128]{2,1,0:T(8,128)S(1)} %get-tuple-element.127), channel_id=1, source_target_pairs={{0,0},{1,2},{2,1},{3,3},{4,4},{5,6},{6,5},{7,7},{8,8},{9,10},{10,9... | collective-permute-start | bytes 786440 | tf_op jit(solution)/shard_map/ppermute | solution.py:337
  35.1 10.5 %collective-permute-start.9 = (f32[16,32,128]{2,1,0:T(8,128)S(1)}, f32[16,32,128]{2,1,0:T(8,128)S(1)}, u32[]{:S(2)}, u32[]{:S(2)}) collective-permute-start(f32[16,32,128]{2,1,0:T(8,128)S(1)} %get-tuple-element.128), channel_id=1, source_target_pairs={{1,0},{0,2},{2,3},{3,1},{5,4},{4,6},{6,7},{7,5},{9,8},{8,10},{10,1... | collective-permute-start | bytes 786440 | tf_op jit(solution)/shard_map/ppermute | solution.py:337
  60.3 8.9 %collective-permute-start.13 = (f32[16,64,128]{2,1,0:T(8,128)S(1)}, f32[16,64,128]{2,1,0:T(8,128)S(1)}, u32[]{:S(2)}, u32[]{:S(2)}) collective-permute-start(f32[16,64,128]{2,1,0:T(8,128)S(1)} %get-tuple-element.75.own_ref), channel_id=1, source_target_pairs={{1,4},{4,1},{5,8},{8,5},{9,12},{12,9},{0,2},{13,15},{3,6},{6,3},{7... | collective-permute-start | bytes 1572872 | tf_op jit(solution)/shard_map/ppermute | solution.py:337
  71.7 8.9 %collective-permute-start.15 = (f32[16,64,128]{2,1,0:T(8,128)S(1)}, f32[16,64,128]{2,1,0:T(8,128)S(1)}, u32[]{:S(2)}, u32[]{:S(2)}) collective-permute-start(f32[16,64,128]{2,1,0:T(8,128)S(1)} %shard_map.48.own_ref), channel_id=1, source_target_pairs={{1,4},{4,1},{5,8},{8,5},{9,12},{12,9},{0,2},{13,15},{3,6},{6,3},{7... | collective-permute-start | bytes 1572872 | tf_op jit(solution)/shard_map/ppermute | solution.py:337
  91.4 15.0 %collective-permute-start.17 = (f32[16,64,128]{2,1,0:T(8,128)S(1)}, f32[16,64,128]{2,1,0:T(8,128)S(1)}, u32[]{:S(2)}, u32[]{:S(2)}) collective-permute-start(f32[16,64,128]{2,1,0:T(8,128)S(1)} %get-tuple-element.81.own_ref), channel_id=1, source_target_pairs={{0,1},{1,0},{2,3},{3,2},{4,5},{5,4},{6,7},{7,6},{8,9},{9,8},{10,11... | collective-permute-start | bytes 1572872 | tf_op jit(solution)/shard_map/ppermute | solution.py:337
  92.6 13.7 %collective-permute-start.18 = (f32[16,64,128]{2,1,0:T(8,128)S(1)}, f32[16,64,128]{2,1,0:T(8,128)S(1)}, u32[]{:S(2)}, u32[]{:S(2)}) collective-permute-start(f32[16,64,128]{2,1,0:T(8,128)S(1)} %get-tuple-element.81.own_ref), channel_id=1, source_target_pairs={{1,4},{4,1},{5,8},{8,5},{9,12},{12,9},{0,2},{13,15},{3,6},{6,3},{7... | collective-permute-start | bytes 1572872 | tf_op jit(solution)/shard_map/ppermute | solution.py:337
  92.7 7.9 %collective-permute-start.19 = (f32[16,32,128]{2,1,0:T(8,128)S(1)}, f32[16,32,128]{2,1,0:T(8,128)S(1)}, u32[]{:S(2)}, u32[]{:S(2)}) collective-permute-start(f32[16,32,128]{2,1,0:T(8,128)S(1)} %get-tuple-element.126), channel_id=1, source_target_pairs={{1,0},{0,2},{2,3},{3,1},{5,4},{4,6},{6,7},{7,5},{9,8},{8,10},{10,1... | collective-permute-start | bytes 786440 | tf_op jit(solution)/shard_map/ppermute | solution.py:337
  93.1 13.3 %collective-permute-start.20 = (f32[16,32,128]{2,1,0:T(8,128)S(1)}, f32[16,32,128]{2,1,0:T(8,128)S(1)}, u32[]{:S(2)}, u32[]{:S(2)}) collective-permute-start(f32[16,32,128]{2,1,0:T(8,128)S(1)} %get-tuple-element.125), channel_id=1, source_target_pairs={{0,0},{1,2},{2,1},{3,3},{4,4},{5,6},{6,5},{7,7},{8,8},{9,10},{10,9... | collective-permute-start | bytes 786440 | tf_op jit(solution)/shard_map/ppermute | solution.py:337
  108.4 9.0 %collective-permute-start.22 = (f32[16,64,128]{2,1,0:T(8,128)S(1)}, f32[16,64,128]{2,1,0:T(8,128)S(1)}, u32[]{:S(2)}, u32[]{:S(2)}) collective-permute-start(f32[16,64,128]{2,1,0:T(8,128)S(1)} %shard_map.51.own_ref), channel_id=1, source_target_pairs={{1,4},{4,1},{5,8},{8,5},{9,12},{12,9},{0,2},{13,15},{3,6},{6,3},{7... | collective-permute-start | bytes 1572872 | tf_op jit(solution)/shard_map/ppermute | solution.py:337
  129.7 8.9 %collective-permute-start.25 = (f32[16,64,128]{2,1,0:T(8,128)S(1)}, f32[16,64,128]{2,1,0:T(8,128)S(1)}, u32[]{:S(2)}, u32[]{:S(2)}) collective-permute-start(f32[16,64,128]{2,1,0:T(8,128)S(1)} %get-tuple-element.87.own_ref), channel_id=1, source_target_pairs={{1,4},{4,1},{5,8},{8,5},{9,12},{12,9},{0,2},{13,15},{3,6},{6,3},{7... | collective-permute-start | bytes 1572872 | tf_op jit(solution)/shard_map/ppermute | solution.py:337
  141.0 8.9 %collective-permute-start.27 = (f32[16,64,128]{2,1,0:T(8,128)S(1)}, f32[16,64,128]{2,1,0:T(8,128)S(1)}, u32[]{:S(2)}, u32[]{:S(2)}) collective-permute-start(f32[16,64,128]{2,1,0:T(8,128)S(1)} %shard_map.54.own_ref), channel_id=1, source_target_pairs={{1,4},{4,1},{5,8},{8,5},{9,12},{12,9},{0,2},{13,15},{3,6},{6,3},{7... | collective-permute-start | bytes 1572872 | tf_op jit(solution)/shard_map/ppermute | solution.py:337
  160.7 15.0 %collective-permute-start.29 = (f32[16,64,128]{2,1,0:T(8,128)S(1)}, f32[16,64,128]{2,1,0:T(8,128)S(1)}, u32[]{:S(2)}, u32[]{:S(2)}) collective-permute-start(f32[16,64,128]{2,1,0:T(8,128)S(1)} %get-tuple-element.93.own_ref), channel_id=1, source_target_pairs={{0,1},{1,0},{2,3},{3,2},{4,5},{5,4},{6,7},{7,6},{8,9},{9,8},{10,11... | collective-permute-start | bytes 1572872 | tf_op jit(solution)/shard_map/ppermute | solution.py:337
  162.0 13.7 %collective-permute-start.30 = (f32[16,64,128]{2,1,0:T(8,128)S(1)}, f32[16,64,128]{2,1,0:T(8,128)S(1)}, u32[]{:S(2)}, u32[]{:S(2)}) collective-permute-start(f32[16,64,128]{2,1,0:T(8,128)S(1)} %get-tuple-element.93.own_ref), channel_id=1, source_target_pairs={{1,4},{4,1},{5,8},{8,5},{9,12},{12,9},{0,2},{13,15},{3,6},{6,3},{7... | collective-permute-start | bytes 1572872 | tf_op jit(solution)/shard_map/ppermute | solution.py:337
  162.0 7.9 %collective-permute-start.31 = (f32[16,32,128]{2,1,0:T(8,128)S(1)}, f32[16,32,128]{2,1,0:T(8,128)S(1)}, u32[]{:S(2)}, u32[]{:S(2)}) collective-permute-start(f32[16,32,128]{2,1,0:T(8,128)S(1)} %get-tuple-element.124), channel_id=1, source_target_pairs={{1,0},{0,2},{2,3},{3,1},{5,4},{4,6},{6,7},{7,5},{9,8},{8,10},{10,1... | collective-permute-start | bytes 786440 | tf_op jit(solution)/shard_map/ppermute | solution.py:337
  163.5 12.2 %collective-permute-start.32 = (f32[16,32,128]{2,1,0:T(8,128)S(1)}, f32[16,32,128]{2,1,0:T(8,128)S(1)}, u32[]{:S(2)}, u32[]{:S(2)}) collective-permute-start(f32[16,32,128]{2,1,0:T(8,128)S(1)} %get-tuple-element.123), channel_id=1, source_target_pairs={{0,0},{1,2},{2,1},{3,3},{4,4},{5,6},{6,5},{7,7},{8,8},{9,10},{10,9... | collective-permute-start | bytes 786440 | tf_op jit(solution)/shard_map/ppermute | solution.py:337
  177.8 9.0 %collective-permute-start.34 = (f32[16,64,128]{2,1,0:T(8,128)S(1)}, f32[16,64,128]{2,1,0:T(8,128)S(1)}, u32[]{:S(2)}, u32[]{:S(2)}) collective-permute-start(f32[16,64,128]{2,1,0:T(8,128)S(1)} %shard_map.57.own_ref), channel_id=1, source_target_pairs={{1,4},{4,1},{5,8},{8,5},{9,12},{12,9},{0,2},{13,15},{3,6},{6,3},{7... | collective-permute-start | bytes 1572872 | tf_op jit(solution)/shard_map/ppermute | solution.py:337
  199.5 8.9 %collective-permute-start.37 = (f32[16,64,128]{2,1,0:T(8,128)S(1)}, f32[16,64,128]{2,1,0:T(8,128)S(1)}, u32[]{:S(2)}, u32[]{:S(2)}) collective-permute-start(f32[16,64,128]{2,1,0:T(8,128)S(1)} %get-tuple-element.99.own_ref), channel_id=1, source_target_pairs={{1,4},{4,1},{5,8},{8,5},{9,12},{12,9},{0,2},{13,15},{3,6},{6,3},{7... | collective-permute-start | bytes 1572872 | tf_op jit(solution)/shard_map/ppermute | solution.py:337
  211.0 8.9 %collective-permute-start.39 = (f32[16,64,128]{2,1,0:T(8,128)S(1)}, f32[16,64,128]{2,1,0:T(8,128)S(1)}, u32[]{:S(2)}, u32[]{:S(2)}) collective-permute-start(f32[16,64,128]{2,1,0:T(8,128)S(1)} %shard_map.60.own_ref), channel_id=1, source_target_pairs={{1,4},{4,1},{5,8},{8,5},{9,12},{12,9},{0,2},{13,15},{3,6},{6,3},{7... | collective-permute-start | bytes 1572872 | tf_op jit(solution)/shard_map/ppermute | solution.py:337
  230.7 15.0 %collective-permute-start.41 = (f32[16,64,128]{2,1,0:T(8,128)S(1)}, f32[16,64,128]{2,1,0:T(8,128)S(1)}, u32[]{:S(2)}, u32[]{:S(2)}) collective-permute-start(f32[16,64,128]{2,1,0:T(8,128)S(1)} %get-tuple-element.105.own_ref), channel_id=1, source_target_pairs={{0,1},{1,0},{2,3},{3,2},{4,5},{5,4},{6,7},{7,6},{8,9},{9,8},{10,11... | collective-permute-start | bytes 1572872 | tf_op jit(solution)/shard_map/ppermute | solution.py:337
  232.0 13.7 %collective-permute-start.42 = (f32[16,64,128]{2,1,0:T(8,128)S(1)}, f32[16,64,128]{2,1,0:T(8,128)S(1)}, u32[]{:S(2)}, u32[]{:S(2)}) collective-permute-start(f32[16,64,128]{2,1,0:T(8,128)S(1)} %get-tuple-element.105.own_ref), channel_id=1, source_target_pairs={{1,4},{4,1},{5,8},{8,5},{9,12},{12,9},{0,2},{13,15},{3,6},{6,3},{7... | collective-permute-start | bytes 1572872 | tf_op jit(solution)/shard_map/ppermute | solution.py:337
  232.1 8.0 %collective-permute-start.43 = (f32[16,32,128]{2,1,0:T(8,128)S(1)}, f32[16,32,128]{2,1,0:T(8,128)S(1)}, u32[]{:S(2)}, u32[]{:S(2)}) collective-permute-start(f32[16,32,128]{2,1,0:T(8,128)S(1)} %get-tuple-element.122), channel_id=1, source_target_pairs={{1,0},{0,2},{2,3},{3,1},{5,4},{4,6},{6,7},{7,5},{9,8},{8,10},{10,1... | collective-permute-start | bytes 786440 | tf_op jit(solution)/shard_map/ppermute | solution.py:337
  233.9 11.8 %collective-permute-start.44 = (f32[16,32,128]{2,1,0:T(8,128)S(1)}, f32[16,32,128]{2,1,0:T(8,128)S(1)}, u32[]{:S(2)}, u32[]{:S(2)}) collective-permute-start(f32[16,32,128]{2,1,0:T(8,128)S(1)} %get-tuple-element.121), channel_id=1, source_target_pairs={{0,0},{1,2},{2,1},{3,3},{4,4},{5,6},{6,5},{7,7},{8,8},{9,10},{10,9... | collective-permute-start | bytes 786440 | tf_op jit(solution)/shard_map/ppermute | solution.py:337
  248.2 8.9 %collective-permute-start.46 = (f32[16,64,128]{2,1,0:T(8,128)S(1)}, f32[16,64,128]{2,1,0:T(8,128)S(1)}, u32[]{:S(2)}, u32[]{:S(2)}) collective-permute-start(f32[16,64,128]{2,1,0:T(8,128)S(1)} %shard_map.63.own_ref), channel_id=1, source_target_pairs={{1,4},{4,1},{5,8},{8,5},{9,12},{12,9},{0,2},{13,15},{3,6},{6,3},{7... | collective-permute-start | bytes 1572872 | tf_op jit(solution)/shard_map/ppermute | solution.py:337
  269.9 8.9 %collective-permute-start.49 = (f32[16,64,128]{2,1,0:T(8,128)S(1)}, f32[16,64,128]{2,1,0:T(8,128)S(1)}, u32[]{:S(2)}, u32[]{:S(2)}) collective-permute-start(f32[16,64,128]{2,1,0:T(8,128)S(1)} %get-tuple-element.111.own_ref), channel_id=1, source_target_pairs={{1,4},{4,1},{5,8},{8,5},{9,12},{12,9},{0,2},{13,15},{3,6},{6,3},{7... | collective-permute-start | bytes 1572872 | tf_op jit(solution)/shard_map/ppermute | solution.py:337
  281.2 8.9 %collective-permute-start.51 = (f32[16,64,128]{2,1,0:T(8,128)S(1)}, f32[16,64,128]{2,1,0:T(8,128)S(1)}, u32[]{:S(2)}, u32[]{:S(2)}) collective-permute-start(f32[16,64,128]{2,1,0:T(8,128)S(1)} %shard_map.66.own_ref), channel_id=1, source_target_pairs={{1,4},{4,1},{5,8},{8,5},{9,12},{12,9},{0,2},{13,15},{3,6},{6,3},{7... | collective-permute-start | bytes 1572872 | tf_op jit(solution)/shard_map/ppermute | solution.py:337
  298.7 8.5 %collective-permute-start.53 = (f32[16,32,128]{2,1,0:T(8,128)S(1)}, f32[16,32,128]{2,1,0:T(8,128)S(1)}, u32[]{:S(2)}, u32[]{:S(2)}) collective-permute-start(f32[16,32,128]{2,1,0:T(8,128)S(1)} %get-tuple-element.115), channel_id=1, source_target_pairs={{0,0},{2,1},{1,2},{3,3},{4,4},{6,5},{5,6},{7,7},{8,8},{10,9},{9,10... | collective-permute-start | bytes 786440 | tf_op jit(solution)/shard_map/ppermute | solution.py:337
  (28 other events, 168.7 us)
